TPU v7x, 256 devices: a whole 4x4x8 slice. The times are simulated.
256 devices in a mesh: paper: 64 (over z, y, core), author: 4 (over x).
Axes of the slice: x: 4, y: 4, z: 8, core: 2. Of those that a mesh axis runs over, the one named last changes fastest.
Arguments:
- paper_feat: bfloat16 [16384, 1024], P('paper', 'author'), may hold values from -6 to 6
- author_feat: bfloat16 [16384, 1024], P('paper', 'author'), may hold values from -6 to 6
- cite_owner: int32 [3072, 1], P('paper'), may hold values from 0 to 63; in each aligned block of 48 rows (0 to 47, 48 to 95, ...) no two rows name the same one
- cite_source: int32 [3072], P('paper'), may hold values from 0 to 1
- cite_target: int32 [3072], P('paper'), may hold values from 0 to 1
- cite_edges: int32 [3072], P('paper'), may hold values from 8 to 64
- cite_count: int32 [64], P('paper'), may hold values from 36 to 48, as said below
- citation_weight_tiles: bfloat16 [3072, 128, 128], P('paper'), may hold values from 0 to 1
- write_owner: int32 [2048, 1], P('paper'), may hold values from 0 to 63; in each aligned block of 32 rows (0 to 31, 32 to 63, ...) no two rows name the same one
- write_paper: int32 [2048], P('paper'), may hold values from 0 to 1
- write_author: int32 [2048], P('paper'), may hold values from 0 to 1
- write_edges: int32 [2048], P('paper'), may hold values from 8 to 64
- authorship_weight_tiles: bfloat16 [2048, 128, 128], P('paper'), may hold values from 0 to 1
- w_self: bfloat16 [1024, 1024], replicated, may hold values from -0.1875 to 0.1875
- w_cite: bfloat16 [1024, 1024], replicated, may hold values from -0.1875 to 0.1875
- w_write: bfloat16 [1024, 1024], replicated, may hold values from -0.1875 to 0.1875
- cotangent: bfloat16 [16384, 1024], P('paper', 'author'), may hold values from -6 to 6
Outputs:
- paper_out: bfloat16 [16384, 1024], P('paper', 'author')
- paper_grad: bfloat16 [16384, 1024], P('paper', 'author')
- author_grad: bfloat16 [16384, 1024], P('paper', 'author')
Inputs may be any that keep to these rules, and one draw needn't show every extreme that they name: `cite_owner`: among the 48 tiles of one paper index (live or not), at most 1 have their source on any one paper index. The live tiles of a paper index are the first cite_count of its list; some paper index has all 48 live. `write_owner`: among the 32 tiles of one paper index, at most 1 take their author block from any one paper index.
All inputs are finite; a program needn't handle non-finite values.
Results may differ from a plain program's by a relative error of at most 0.007.
Values may be sent and summed in bfloat16 or wider, within the bound.
A program may use at most 128 MiB of HBM per device.

v0:
```python
import jax
import jax.numpy as jnp
from jax import lax
from jax.sharding import PartitionSpec as P

TOP_PRECISION = lax.Precision.HIGHEST


def silu_slope(values):
    sigma = jax.nn.sigmoid(values)
    return sigma * (1.0 + values * (1.0 - sigma))


def matmul(left, right):
    return jnp.dot(left, right, preferred_element_type=jnp.float32)


def matmul_flipped(left, right):
    return lax.dot_general(
        left, right, (((1,), (1,)), ((), ())), preferred_element_type=jnp.float32
    )


def slot_layout(owners, slot_count, slot_total):
    count = owners.shape[0]
    order = jnp.arange(count, dtype=jnp.int32)
    earlier = (owners[:, None] == owners[None, :]) & (order[:, None] > order[None, :])
    rank = jnp.sum(earlier.astype(jnp.int32), axis=1)
    position = owners * slot_count + rank
    positioned_rows = position[:, None] == jnp.arange(slot_total, dtype=jnp.int32)[None, :]
    return (position, positioned_rows)


def body(
    paper_feat,
    author_feat,
    cite_owner,
    cite_source,
    cite_target,
    cite_edges,
    cite_count,
    citation_weight_tiles,
    write_owner,
    write_paper,
    write_author,
    write_edges,
    authorship_weight_tiles,
    w_self,
    w_cite,
    w_write,
    cotangent,
):
    peer_count = lax.axis_size("paper")
    tile_total = citation_weight_tiles.shape[0]
    tile_rows = citation_weight_tiles.shape[1]
    paper_rows, quarter = paper_feat.shape
    author_rows = author_feat.shape[0]
    paper_blocks = paper_rows // tile_rows
    author_blocks = author_rows // tile_rows
    slot_count = tile_total // peer_count + 1
    slot_total = peer_count * slot_count
    write_total = authorship_weight_tiles.shape[0]
    wslot_count = write_total // peer_count + 1
    wslot_total = peer_count * wslot_count
    block_range = jnp.arange(paper_blocks, dtype=jnp.int32)
    author_range = jnp.arange(author_blocks, dtype=jnp.int32)
    position, positioned_rows = slot_layout(cite_owner[:, 0], slot_count, slot_total)
    tile_order = jnp.arange(tile_total, dtype=jnp.int32)
    wanted = jnp.sum(jnp.where(positioned_rows, cite_source[:, None], 0), axis=0)
    incoming_ids = lax.all_to_all(
        wanted.reshape(peer_count, slot_count), "paper", split_axis=0, concat_axis=0, tiled=True
    )
    live_tile = tile_order < cite_count[0]
    tile_scale = jnp.where(live_tile, 1.0 / cite_edges.astype(jnp.float32), 0.0)
    target_hot = jnp.where(cite_target[:, None] == block_range[None, :], tile_scale[:, None], 0.0)
    slotted_weight_tiles = jnp.einsum(
        "tk,tab->kab",
        positioned_rows.astype(jnp.bfloat16),
        citation_weight_tiles,
        preferred_element_type=jnp.float32,
    ).astype(jnp.bfloat16)
    slotted_target_index = jnp.einsum(
        "tk,tp->kp", positioned_rows.astype(jnp.float32), target_hot, precision=TOP_PRECISION
    )
    pieces = lax.all_gather(paper_feat, "paper", axis=0, tiled=True)
    shard_count = pieces.shape[0] // paper_rows
    span = shard_count * slot_count
    shard_of = jnp.arange(span, dtype=jnp.int32) // slot_count
    stacked = pieces.reshape(shard_count * paper_blocks, tile_rows, quarter)
    selected_rows = jnp.take(stacked, shard_of * paper_blocks + wanted, axis=0)
    partial_block_value = jnp.einsum(
        "eih,ehp->eip", slotted_weight_tiles, selected_rows, preferred_element_type=jnp.float32
    )
    citation_accumulator = jnp.einsum(
        "nr,nmh->rmh", slotted_target_index, partial_block_value, precision=TOP_PRECISION
    )
    cite_sum = citation_accumulator.reshape(paper_rows, quarter).astype(jnp.bfloat16)
    wposition, wplaced = slot_layout(write_owner[:, 0], wslot_count, wslot_total)
    wanted_authors = jnp.sum(jnp.where(wplaced, write_author[:, None], 0), axis=0)
    author_ids = lax.all_to_all(
        wanted_authors.reshape(peer_count, wslot_count),
        "paper",
        split_axis=0,
        concat_axis=0,
        tiled=True,
    )
    author_stack = author_feat.reshape(author_blocks, tile_rows, quarter)
    author_out = jnp.take(author_stack, author_ids.reshape(-1), axis=0).reshape(
        peer_count, wslot_count, tile_rows, quarter
    )
    author_in = lax.all_to_all(author_out, "paper", split_axis=0, concat_axis=0, tiled=True)
    write_scale = 1.0 / write_edges.astype(jnp.float32)
    authorship_sources = jnp.take(
        author_in.reshape(wslot_total, tile_rows, quarter), wposition, axis=0
    )
    authorship_products = jnp.einsum(
        "eih,ehp->eip",
        authorship_weight_tiles,
        authorship_sources,
        preferred_element_type=jnp.float32,
    )
    paper_onehot_mask = jnp.where(
        write_paper[:, None] == block_range[None, :], write_scale[:, None], 0.0
    )
    authorship_sum = jnp.einsum(
        "nr,nmh->rmh", paper_onehot_mask, authorship_products, precision=TOP_PRECISION
    )
    authorship_sum = authorship_sum.reshape(paper_rows, quarter).astype(jnp.bfloat16)
    column = lax.axis_index("author") * quarter
    feats = lax.all_gather(paper_feat, "author", axis=1, tiled=True)
    cites = lax.all_gather(cite_sum, "author", axis=1, tiled=True)
    writes = lax.all_gather(authorship_sum, "author", axis=1, tiled=True)
    span = feats.shape[1]

    def window(weight):
        return lax.dynamic_slice(weight, (0, column), (span, quarter))

    preact = (
        matmul(feats, window(w_self))
        + matmul(cites, window(w_cite))
        + matmul(writes, window(w_write))
    )
    paper_out = (paper_feat.astype(jnp.float32) + jax.nn.silu(preact)).astype(jnp.bfloat16)
    grad_pre = (cotangent.astype(jnp.float32) * silu_slope(preact)).astype(jnp.bfloat16)
    pieces = lax.all_gather(grad_pre, "author", axis=1, tiled=True)
    fold_span = pieces.shape[1]

    def flipped(weight):
        return matmul_flipped(pieces, lax.dynamic_slice(weight, (column, 0), (quarter, fold_span)))

    self_back = flipped(w_self)
    cite_back = flipped(w_cite)
    write_back = flipped(w_write)
    cite_grad = cite_back.astype(jnp.bfloat16).reshape(paper_blocks, tile_rows, quarter)
    target_indices = jnp.take(cite_grad, cite_target, axis=0)
    returned_rows = jnp.einsum(
        "pdg,pdw->pgw", citation_weight_tiles, target_indices, preferred_element_type=jnp.float32
    )
    returned_rows = (returned_rows * tile_scale[:, None, None]).astype(jnp.bfloat16)
    outgoing_grad = jnp.einsum(
        "hs,hip->sip",
        positioned_rows.astype(jnp.bfloat16),
        returned_rows,
        preferred_element_type=jnp.float32,
    )
    outgoing_grad = outgoing_grad.astype(jnp.bfloat16).reshape(
        peer_count, slot_count, tile_rows, quarter
    )
    arrived = lax.all_to_all(outgoing_grad, "paper", split_axis=0, concat_axis=0, tiled=True)
    arrived_hot = (incoming_ids.reshape(-1)[:, None] == block_range[None, :]).astype(jnp.bfloat16)
    cite_return = jnp.einsum(
        "kp,kac->pac",
        arrived_hot,
        arrived.reshape(slot_total, tile_rows, quarter),
        preferred_element_type=jnp.float32,
    )
    paper_grad = (
        cotangent.astype(jnp.float32) + self_back + cite_return.reshape(paper_rows, quarter)
    ).astype(jnp.bfloat16)
    write_grad = write_back.astype(jnp.bfloat16).reshape(paper_blocks, tile_rows, quarter)
    authorship_targets = jnp.take(write_grad, write_paper, axis=0)
    author_products = jnp.einsum(
        "pdg,pdw->pgw",
        authorship_weight_tiles,
        authorship_targets,
        preferred_element_type=jnp.float32,
    )
    author_products = (author_products * write_scale[:, None, None]).astype(jnp.bfloat16)
    author_send = jnp.einsum(
        "hs,hip->sip",
        wplaced.astype(jnp.bfloat16),
        author_products,
        preferred_element_type=jnp.float32,
    )
    author_send = author_send.astype(jnp.bfloat16).reshape(
        peer_count, wslot_count, tile_rows, quarter
    )
    author_back = lax.all_to_all(author_send, "paper", split_axis=0, concat_axis=0, tiled=True)
    author_hot = (author_ids.reshape(-1)[:, None] == author_range[None, :]).astype(jnp.bfloat16)
    author_grad = jnp.einsum(
        "kp,kac->pac",
        author_hot,
        author_back.reshape(wslot_total, tile_rows, quarter),
        preferred_element_type=jnp.float32,
    )
    author_grad = author_grad.reshape(author_rows, quarter).astype(jnp.bfloat16)
    return (paper_out, paper_grad, author_grad)


def solution(mesh):
    in_specs = (
        P("paper", "author"),
        P("paper", "author"),
        P("paper", None),
        P("paper"),
        P("paper"),
        P("paper"),
        P("paper"),
        P("paper", None, None),
        P("paper", None),
        P("paper"),
        P("paper"),
        P("paper"),
        P("paper", None, None),
        P(),
        P(),
        P(),
        P("paper", "author"),
    )
    out_specs = (P("paper", "author"), P("paper", "author"), P("paper", "author"))
    return jax.shard_map(body, mesh=mesh, in_specs=in_specs, out_specs=out_specs, check_vma=False)
```

profile of v0, /device:TPU:2, one launch (start us, length us, event | category | flops | bytes accessed | tf_op | source)
XLA Modules:
  0.0 490.8 jit_solution(11593306411064109347)
XLA Ops:
  10.3 21.5 %all_to_all.39 = s32[64,1,1]{2,1,0:T(1,128)S(1)} all-to-all(s32[64,1,1]{2,1,0:T(1,128)S(1)} %copy.96), channel_id=1, replica_groups=mesh['paper'=64,'author'=4] {'paper'}, dimensions={0} | all-to-all | bytes 512 | tf_op jit(solution)/shard_map/all_to_all | solution.py:100
  35.9 4.6 bitcast_select_fusion
  40.5 5.8 %all-to-all-start.1 = ((bf16[64,1,128,256]{3,2,1,0:T(8,128)(2,1)}), bf16[64,1,128,256]{3,2,1,0:T(8,128)(2,1)}, u32[]{:S(2)}, u32[]{:S(2)}) async-start(bf16[64,1,128,256]{3,2,1,0:T(8,128)(2,1)} %bitcast_select_fusion), calls=%async_computation.1 | async-start | bytes 8388608 | tf_op jit(solution)/shard_map/all_to_all | solution.py:111
  48.8 13.0 %all_gather.15 = bf16[256,1024]{1,0:T(8,128)(2,1)S(1)} all-gather(bf16[256,256]{1,0:T(8,128)(2,1)S(1)} %copy-done.2), channel_id=1, replica_groups=mesh['paper'=64,'author'=4] {'author'}, dimensions={1}, use_global_device_ids=true | all-gather | bytes 655360 | tf_op jit(solution)/shard_map/all_gather | solution.py:130
  62.4 4.2 convolution_convert_fusion
  66.6 96.0 %all-to-all-done.1 = bf16[64,1,128,256]{3,2,1,0:T(8,128)(2,1)} async-done(((bf16[64,1,128,256]{3,2,1,0:T(8,128)(2,1)}), bf16[64,1,128,256]{3,2,1,0:T(8,128)(2,1)}, u32[]{:S(2)}, u32[]{:S(2)}) %all-to-all-start.1) | async-done | bytes 4194336 | tf_op jit(solution)/shard_map/all_to_all | solution.py:111
  162.6 5.4 %all-to-all-start.2 = ((s32[64,1,1]{2,1,0:T(1,128)}), s32[64,1,1]{2,1,0:T(1,128)}, u32[]{:S(2)}, u32[]{:S(2)}) async-start(s32[64,1,1]{2,1,0:T(1,128)} %copy.103), calls=%async_computation.2 | async-start | bytes 65536 | tf_op jit(solution)/shard_map/all_to_all | solution.py:70
  168.1 4.2 gather_fusion.2
  172.3 4.6 convolution_bitcast_fusion
  176.9 5.5 %copy.98 = f32[32,128,256]{2,0,1:T(8,128)} copy(f32[32,128,256]{1,2,0:T(8,128)} %convolution_bitcast_fusion) | data formatting | bytes 8388608 | tf_op jit(solution)/shard_map/eih,ehp->eip/dot_general | solution.py:116
  182.4 4.3 convolution_convert_fusion.3
  186.7 13.9 %all_gather.18 = bf16[256,1024]{1,0:T(8,128)(2,1)S(1)} all-gather(bf16[256,256]{1,0:T(8,128)(2,1)S(1)} %bitcast.106), channel_id=1, replica_groups=mesh['paper'=64,'author'=4] {'author'}, dimensions={1}, use_global_device_ids=true | all-gather | bytes 655360 | tf_op jit(solution)/shard_map/all_gather | solution.py:132
  200.6 6.2 %gather_fusion = bf16[64,128,256]{2,1,0:T(8,128)(2,1)} fusion(bf16[128,128,256]{2,1,0:T(8,128)(2,1)} %bitcast.104, s32[1024]{0:T(1024)S(1)} %pad_clamp_fusion.4), kind=kCustom, calls=%fused_computation | custom fusion | bytes 8388864 | tf_op jit(solution)/shard_map/jit(_take)/gather | solution.py:90
  206.8 5.1 %fusion.5 = f32[64,128,256]{2,1,0:T(8,128)S(1)} fusion(bf16[64,128,256]{2,1,0:T(8,128)(2,1)} %gather_fusion, pred[64]{0:T(512)(128)(4,1)S(1)} %compare_and_fusion.3, bf16[64,128,128]{2,0,1:T(8,128)(2,1)} %convolution_convert_fusion), kind=kOutput, calls=%fused_computation.15 | convolution fusion | flops 538968064 | bytes 14680128 | tf_op jit(solution)/shard_map/eih,ehp->eip/dot_general | solution.py:91
  211.9 8.6 %fusion.31 = bf16[2,128,256]{2,0,1:T(2,128)(2,1)S(1)} fusion(f32[64,2,1]{0,1,2:T(2,128)S(1)} %convolution_bitcast_fusion.2, f32[64,128,256]{2,1,0:T(8,128)S(1)} %fusion.5), kind=kOutput, calls=%fused_computation.42 | convolution fusion | flops 50397184 | bytes 8520192 | tf_op jit(solution)/shard_map/nr,nmh->rmh/dot_general | solution.py:94
  220.5 13.3 %all_gather.17 = bf16[256,1024]{1,0:T(8,128)(2,1)S(1)} all-gather(bf16[256,256]{1,0:T(8,128)(2,1)S(1)} %bitcast.107), channel_id=1, replica_groups=mesh['paper'=64,'author'=4] {'author'}, dimensions={1}, use_global_device_ids=true | all-gather | bytes 655360 | tf_op jit(solution)/shard_map/all_gather | solution.py:131
  236.1 12.8 %all_gather.19 = bf16[256,1024]{0,1:T(8,128)(2,1)S(1)} all-gather(bf16[256,256]{0,1:T(8,128)(2,1)S(1)} %get-tuple-element.20), channel_id=1, replica_groups=mesh['paper'=64,'author'=4] {'author'}, dimensions={1}, use_global_device_ids=true | all-gather | bytes 655360 | tf_op jit(solution)/shard_map/all_gather | solution.py:145
  251.8 5.5 %fusion.8 = bf16[48,128,256]{1,2,0:T(8,128)(2,1)} fusion(f32[48]{0:T(128)S(1)} %copy-done.17, bf16[48,128,128]{2,1,0:T(8,128)(2,1)} %param.24, bf16[48,128,256]{2,1,0:T(8,128)(2,1)} %gather_fusion.3, pred[48]{0:T(512)(128)(4,1)S(1)} %copy-done.18), kind=kOutput, calls=%fused_computation.18 | convolution fusion | flops 407371776 | bytes 7864560 | tf_op jit(solution)/shard_map/pdg,pdw->pgw/dot_general | solution.py:156
  257.3 4.9 %copy.105 = bf16[48,128,256]{2,0,1:T(8,128)(2,1)} copy(bf16[48,128,256]{1,2,0:T(8,128)(2,1)} %fusion.8) | data formatting | bytes 6291456 | tf_op jit(solution)/shard_map/convert_element_type | solution.py:159
  262.2 3.2 convert_bitcast_fusion.1
  265.4 4.4 copy.106
  269.8 10.6 %all-to-all-start.3 = ((bf16[64,1,128,256]{3,2,1,0:T(8,128)(2,1)}), bf16[64,1,128,256]{3,2,1,0:T(8,128)(2,1)}, u32[]{:S(2)}, u32[]{:S(2)}) async-start(bf16[64,1,128,256]{3,2,1,0:T(8,128)(2,1)} %copy.106), calls=%async_computation.3 | async-start | bytes 8388608 | tf_op jit(solution)/shard_map/all_to_all | solution.py:169
  282.9 4.3 fusion.20
  287.2 4.6 copy.110
  291.8 2.9 convert_bitcast_fusion
  294.7 4.4 copy.111
  299.1 77.5 %all-to-all-done.3 = bf16[64,1,128,256]{3,2,1,0:T(8,128)(2,1)} async-done(((bf16[64,1,128,256]{3,2,1,0:T(8,128)(2,1)}), bf16[64,1,128,256]{3,2,1,0:T(8,128)(2,1)}, u32[]{:S(2)}, u32[]{:S(2)}) %all-to-all-start.3) | async-done | bytes 4194336 | tf_op jit(solution)/shard_map/all_to_all | solution.py:169
  376.6 5.7 %all-to-all-start.4 = ((bf16[64,1,128,256]{3,2,1,0:T(8,128)(2,1)}), bf16[64,1,128,256]{3,2,1,0:T(8,128)(2,1)}, u32[]{:S(2)}, u32[]{:S(2)}) async-start(bf16[64,1,128,256]{3,2,1,0:T(8,128)(2,1)} %copy.111), calls=%async_computation.4 | async-start | bytes 8388608 | tf_op jit(solution)/shard_map/all_to_all | solution.py:198
  385.1 6.5 %copy.121 = bf16[64,128,256]{1,0,2:T(8,128)(2,1)} copy(bf16[64,128,256]{2,1,0:T(8,128)(2,1)} %bitcast.29) | data formatting | bytes 8388608 | tf_op jit(solution)/shard_map/reshape | solution.py:174
  391.6 2.8 fusion.60
  396.6 82.0 %all-to-all-done.4 = bf16[64,1,128,256]{3,2,1,0:T(8,128)(2,1)} async-done(((bf16[64,1,128,256]{3,2,1,0:T(8,128)(2,1)}), bf16[64,1,128,256]{3,2,1,0:T(8,128)(2,1)}, u32[]{:S(2)}, u32[]{:S(2)}) %all-to-all-start.4) | async-done | bytes 4194336 | tf_op jit(solution)/shard_map/all_to_all | solution.py:198
  478.6 4.5 fusion.27
  (85 shorter events, 22.5 us)
Async XLA Ops:
  7.2 228.5 %copy-start = (bf16[1024,1024]{1,0:T(8,128)(2,1)S(1)}, bf16[1024,1024]{1,0:T(8,128)(2,1)}, u32[]{:S(2)}) copy-start(bf16[1024,1024]{1,0:T(8,128)(2,1)} %param.32) | copy-start | bytes 6291460
  7.2 25.9 %copy-start.1 = (bf16[256,256]{1,0:T(8,128)(2,1)S(1)}, bf16[256,256]{1,0:T(8,128)(2,1)}, u32[]{:S(2)}) copy-start(bf16[256,256]{1,0:T(8,128)(2,1)} %param.18) | copy-start | bytes 393220
  7.2 193.4 %all-gather.2.cloned.1.call-start = ((), (), s32[]{:S(2)}) async-start(), calls=%async_computation.5 | async-start | bytes 8519680 | tf_op jit(solution)/shard_map/all_gather | solution.py:85
  9.5 0.7 copy-start.6
  40.4 5.9 %copy-start.2 = (bf16[256,256]{1,0:T(8,128)(2,1)S(1)}, bf16[256,256]{1,0:T(8,128)(2,1)}, u32[]{:S(2)}) copy-start(bf16[256,256]{1,0:T(8,128)(2,1)} %param.17) | copy-start | bytes 393220
  40.4 6.7 %copy-start.4 = (bf16[256,256]{1,0:T(8,128)(2,1)S(1)}, bf16[256,256]{1,0:T(8,128)(2,1)}, u32[]{:S(2)}) copy-start(bf16[256,256]{1,0:T(8,128)(2,1)} %param.33) | copy-start | bytes 393220
  40.4 6.8 %copy-start.11 = (s32[48,1]{0,1:T(1,128)S(1)}, s32[48,1]{0,1:T(1,128)}, u32[]{:S(2)}) copy-start(s32[48,1]{0,1:T(1,128)} %param.19) | copy-start | bytes 580
  40.4 7.0 %copy-start.12 = (s32[48]{0:T(128)S(1)}, s32[48]{0:T(128)}, u32[]{:S(2)}) copy-start(s32[48]{0:T(128)} %param.20) | copy-start | bytes 580
  40.4 7.8 %copy-start.10 = (s32[32,1]{0,1:T(1,128)S(1)}, s32[32,1]{0,1:T(1,128)}, u32[]{:S(2)}) copy-start(s32[32,1]{0,1:T(1,128)} %param.25) | copy-start | bytes 388
  40.5 7.8 %copy-start.14 = (s32[48]{0:T(128)S(1)}, s32[48]{0:T(128)}, u32[]{:S(2)}) copy-start(s32[48]{0:T(128)} %param.21) | copy-start | bytes 580
  40.5 7.8 %copy-start.13 = (s32[48]{0:T(128)S(1)}, s32[48]{0:T(128)}, u32[]{:S(2)}) copy-start(s32[48]{0:T(128)} %param.22) | copy-start | bytes 580
  40.5 21.9 %copy-start.15 = (s32[32]{0:T(128)S(1)}, s32[32]{0:T(128)}, u32[]{:S(2)}) copy-start(s32[32]{0:T(128)} %param.28) | copy-start | bytes 388
  40.5 122.1 %all-to-all-start.1 = ((bf16[64,1,128,256]{3,2,1,0:T(8,128)(2,1)}), bf16[64,1,128,256]{3,2,1,0:T(8,128)(2,1)}, u32[]{:S(2)}, u32[]{:S(2)}) async-start(bf16[64,1,128,256]{3,2,1,0:T(8,128)(2,1)} %bitcast_select_fusion), calls=%async_computation.1 | async-start | bytes 8388608 | tf_op jit(solution)/shard_map/all_to_all | solution.py:111
  48.3 0.5 copy-start.16
  62.4 120.0 %copy-start.8 = (f32[32]{0:T(128)}, f32[32]{0:T(128)S(1)}, u32[]{:S(2)}) copy-start(f32[32]{0:T(128)S(1)} %convert_divide_fusion) | copy-start | bytes 388
  162.6 107.2 %all-to-all-start.2 = ((s32[64,1,1]{2,1,0:T(1,128)}), s32[64,1,1]{2,1,0:T(1,128)}, u32[]{:S(2)}, u32[]{:S(2)}) async-start(s32[64,1,1]{2,1,0:T(1,128)} %copy.103), calls=%async_computation.2 | async-start | bytes 65536 | tf_op jit(solution)/shard_map/all_to_all | solution.py:70
  176.9 5.5 %copy-start.5 = (s32[32]{0:T(128)S(1)}, s32[32]{0:T(128)}, u32[]{:S(2)}) copy-start(s32[32]{0:T(128)} %param.26) | copy-start | bytes 388
  211.9 22.0 %copy-start.3 = (bf16[1024,1024]{1,0:T(8,128)(2,1)S(1)}, bf16[1024,1024]{1,0:T(8,128)(2,1)}, u32[]{:S(2)}) copy-start(bf16[1024,1024]{1,0:T(8,128)(2,1)} %param.31) | copy-start | bytes 6291460
  249.2 2.5 copy-start.17
  249.2 2.5 copy-start.18
  269.8 106.8 %all-to-all-start.3 = ((bf16[64,1,128,256]{3,2,1,0:T(8,128)(2,1)}), bf16[64,1,128,256]{3,2,1,0:T(8,128)(2,1)}, u32[]{:S(2)}, u32[]{:S(2)}) async-start(bf16[64,1,128,256]{3,2,1,0:T(8,128)(2,1)} %copy.106), calls=%async_computation.3 | async-start | bytes 8388608 | tf_op jit(solution)/shard_map/all_to_all | solution.py:169
  280.4 2.5 copy-start.9
  287.2 4.6 copy-start.7
  376.6 101.9 %all-to-all-start.4 = ((bf16[64,1,128,256]{3,2,1,0:T(8,128)(2,1)}), bf16[64,1,128,256]{3,2,1,0:T(8,128)(2,1)}, u32[]{:S(2)}, u32[]{:S(2)}) async-start(bf16[64,1,128,256]{3,2,1,0:T(8,128)(2,1)} %copy.111), calls=%async_computation.4 | async-start | bytes 8388608 | tf_op jit(solution)/shard_map/all_to_all | solution.py:198
Sparse Core Ops, SparseCore 0:
  10.8 133.2 all-gather.1
where the time goes:
time: 499 us; the launch traced here: 491 us
  waiting for transfers between devices  256 us (51%)
  blocking collectives  74.6 us (15%)
  matrix products  54.6 us (11%)
  local copies, waits for them, and re-layouts  51.6 us (10%)
  starting transfers between devices  27.5 us (6%)
  between operations  15.3 us (3%)
  other arithmetic  11 us (2%)
    all_to_all x1, waiting for transfers between devices, body(): lax.all_to_all(author_out, 'paper', split_axis=0, concat_axis=0, tiled=True)  96 us
    all_to_all x1, waiting for transfers between devices, body(): lax.all_to_all(author_send, 'paper', split_axis=0, concat_axis=0, tiled=T...  82 us
    all_to_all x1, waiting for transfers between devices, body(): lax.all_to_all(outgoing_grad, 'paper', split_axis=0, concat_axis=0, tiled...  77.5 us
    all_to_all x1, blocking collectives, body(): lax.all_to_all(wanted_authors.reshape(peer_count, wslot_count), 'paper',...  21.5 us
    all_gather x1, blocking collectives, body(): writes = lax.all_gather(authorship_sum, 'author', axis=1, tiled=True)  13.9 us
    all_gather x1, blocking collectives, body(): cites = lax.all_gather(cite_sum, 'author', axis=1, tiled=True)  13.3 us
    all_gather x1, blocking collectives, body(): feats = lax.all_gather(paper_feat, 'author', axis=1, tiled=True)  13 us
    all_gather x1, blocking collectives, body(): pieces = lax.all_gather(grad_pre, 'author', axis=1, tiled=True)  12.8 us
  transfers between devices with their start and end apart: 5, of which 3 were waited for; matrix products, arithmetic and copies ran while one was open for 23% of the time, Pallas kernels for 0%

commit v1 on v0

--- a/solution.py
+++ b/solution.py
@@ -127,7 +127,14 @@
     )
     authorship_sum = authorship_sum.reshape(paper_rows, quarter).astype(jnp.bfloat16)
     column = lax.axis_index("author") * quarter
-    feats = lax.all_gather(paper_feat, "author", axis=1, tiled=True)
+    ring = [paper_feat]
+    for hop in range(3):
+        ring.append(lax.ppermute(ring[-1], "author", [(dev, (dev + 1) % 4) for dev in range(4)]))
+    feats = jnp.roll(
+        jnp.concatenate(ring[::-1], axis=1),
+        (lax.axis_index("author") + 1) * ring[0].shape[1],
+        axis=1,
+    )
     cites = lax.all_gather(cite_sum, "author", axis=1, tiled=True)
     writes = lax.all_gather(authorship_sum, "author", axis=1, tiled=True)
     span = feats.shape[1]

time: 499 us -> 511 us (1.024)
  starting transfers between devices: 27.5 us -> 42.6 us
  blocking collectives: 74.6 us -> 61 us
  waiting for transfers between devices: 256 us -> 263 us
    all_gather x1 -> x0, blocking collectives: 13 us -> none  [body(): feats = lax.all_gather(paper_feat, 'author', axis=1, tiled=True)]
    all_to_all x1, starting transfers between devices: 5.42 us -> 16.1 us  [body(): lax.all_to_all(wanted.reshape(peer_count, slot_count), 'paper', split_axi...]
    all_to_all x1, waiting for transfers between devices: 82 us -> 89.4 us  [body(): lax.all_to_all(author_send, 'paper', split_axis=0, concat_axis=0, tiled=T...]
    reshape x1 -> x0, local copies, waits for them, and re-layouts: 6.54 us -> none  [body(): arrived.reshape(slot_total, tile_rows, quarter)]
    all_to_all x1, waiting for transfers between devices: 96 us -> 89.9 us  [body(): lax.all_to_all(author_out, 'paper', split_axis=0, concat_axis=0, tiled=True)]
    ppermute x0 -> x3, waiting for transfers between devices: none -> 6.09 us  [body(): lax.ppermute(ring[-1], 'author', [(dev, (dev + 1) % 4) for dev in range(4)])]
  transfers between devices with their start and end apart: 5 -> 8, of which waited for: 3 -> 5; matrix products, arithmetic and copies ran while one was open for 23% -> 23% of each run, Pallas kernels for 0% -> 0%
where the time goes in v1:
time: 511 us; the launch traced here: 503 us
  waiting for transfers between devices  263 us (51%)
  blocking collectives  61 us (12%)
  matrix products  59 us (12%)
  local copies, waits for them, and re-layouts  50.3 us (10%)
  starting transfers between devices  42.6 us (8%)
  between operations  15.5 us (3%)
  other arithmetic  11.9 us (2%)
    all_to_all x1, waiting for transfers between devices, body(): lax.all_to_all(author_out, 'paper', split_axis=0, concat_axis=0, tiled=True)  89.9 us
    all_to_all x1, waiting for transfers between devices, body(): lax.all_to_all(author_send, 'paper', split_axis=0, concat_axis=0, tiled=T...  89.4 us
    all_to_all x1, waiting for transfers between devices, body(): lax.all_to_all(outgoing_grad, 'paper', split_axis=0, concat_axis=0, tiled...  76.6 us
    all_to_all x1, blocking collectives, body(): lax.all_to_all(wanted_authors.reshape(peer_count, wslot_count), 'paper',...  21.5 us
    all_to_all x1, starting transfers between devices, body(): lax.all_to_all(wanted.reshape(peer_count, slot_count), 'paper', split_axi...  16.1 us
    all_gather x1, blocking collectives, body(): writes = lax.all_gather(authorship_sum, 'author', axis=1, tiled=True)  13.4 us
    all_gather x1, blocking collectives, body(): cites = lax.all_gather(cite_sum, 'author', axis=1, tiled=True)  13.4 us
    all_gather x1, blocking collectives, body(): pieces = lax.all_gather(grad_pre, 'author', axis=1, tiled=True)  12.8 us
  transfers between devices with their start and end apart: 8, of which 5 were waited for; matrix products, arithmetic and copies ran while one was open for 23% of the time, Pallas kernels for 0%

profile of v1, /device:TPU:2, one launch (start us, length us, event | category | flops | bytes accessed | tf_op | source)
XLA Modules:
  0.0 503.1 jit_solution(9873591713581740130)
XLA Ops:
  10.3 21.5 %all_to_all.39 = s32[64,1,1]{2,1,0:T(1,128)S(1)} all-to-all(s32[64,1,1]{2,1,0:T(1,128)S(1)} %copy.66), channel_id=1, replica_groups=mesh['paper'=64,'author'=4] {'paper'}, dimensions={0} | all-to-all | bytes 512 | tf_op jit(solution)/shard_map/all_to_all | solution.py:100
  33.1 2.8 gather_fusion.1
  35.9 4.6 bitcast_select_fusion
  40.5 5.8 %all-to-all-start.1 = ((bf16[64,1,128,256]{3,2,1,0:T(8,128)(2,1)}), bf16[64,1,128,256]{3,2,1,0:T(8,128)(2,1)}, u32[]{:S(2)}, u32[]{:S(2)}) async-start(bf16[64,1,128,256]{3,2,1,0:T(8,128)(2,1)} %bitcast_select_fusion), calls=%async_computation.1 | async-start | bytes 8388608 | tf_op jit(solution)/shard_map/all_to_all | solution.py:111
  51.1 4.2 convolution_convert_fusion
  56.7 3.8 collective-permute-done.1
  72.8 89.9 %all-to-all-done.1 = bf16[64,1,128,256]{3,2,1,0:T(8,128)(2,1)} async-done(((bf16[64,1,128,256]{3,2,1,0:T(8,128)(2,1)}), bf16[64,1,128,256]{3,2,1,0:T(8,128)(2,1)}, u32[]{:S(2)}, u32[]{:S(2)}) %all-to-all-start.1) | async-done | bytes 4194336 | tf_op jit(solution)/shard_map/all_to_all | solution.py:111
  162.6 16.1 %all-to-all-start.2 = ((s32[64,1,1]{2,1,0:T(1,128)}), s32[64,1,1]{2,1,0:T(1,128)S(1)}, u32[]{:S(2)}, u32[]{:S(2)}) async-start(s32[64,1,1]{2,1,0:T(1,128)} %copy.70), calls=%async_computation.2 | async-start | bytes 65536 | tf_op jit(solution)/shard_map/all_to_all | solution.py:70
  178.8 4.2 gather_fusion.2
  183.0 4.4 convolution_bitcast_fusion
  187.4 5.5 %copy.68 = f32[32,128,256]{2,0,1:T(8,128)} copy(f32[32,128,256]{1,2,0:T(8,128)} %convolution_bitcast_fusion) | data formatting | bytes 8388608 | tf_op jit(solution)/shard_map/eih,ehp->eip/dot_general | solution.py:116
  192.9 4.3 convolution_convert_fusion.3
  197.2 13.4 %all_gather.14 = bf16[256,1024]{1,0:T(8,128)(2,1)S(1)} all-gather(bf16[256,256]{1,0:T(8,128)(2,1)S(1)} %bitcast.98), channel_id=1, replica_groups=mesh['paper'=64,'author'=4] {'author'}, dimensions={1}, use_global_device_ids=true | all-gather | bytes 655360 | tf_op jit(solution)/shard_map/all_gather | solution.py:139
  212.0 6.2 %gather_fusion = bf16[64,128,256]{2,1,0:T(8,128)(2,1)} fusion(bf16[128,128,256]{2,1,0:T(8,128)(2,1)} %bitcast.96, s32[1024]{0:T(1024)S(1)} %pad_clamp_fusion.4), kind=kCustom, calls=%fused_computation | custom fusion | bytes 8388864 | tf_op jit(solution)/shard_map/jit(_take)/gather | solution.py:90
  218.1 5.1 %fusion.8 = f32[64,128,256]{2,1,0:T(8,128)S(1)} fusion(bf16[64,128,256]{2,1,0:T(8,128)(2,1)} %gather_fusion, pred[64]{0:T(512)(128)(4,1)S(1)} %copy-done.13, bf16[64,128,128]{2,0,1:T(8,128)(2,1)} %convolution_convert_fusion), kind=kOutput, calls=%fused_computation.18 | convolution fusion | flops 538968064 | bytes 14680128 | tf_op jit(solution)/shard_map/eih,ehp->eip/dot_general | solution.py:91
  223.2 8.6 %fusion.34 = bf16[2,128,256]{2,0,1:T(2,128)(2,1)S(1)} fusion(f32[64,2,1]{0,1,2:T(2,128)S(1)} %copy-done.8, f32[64,128,256]{2,1,0:T(8,128)S(1)} %fusion.8), kind=kOutput, calls=%fused_computation.44 | convolution fusion | flops 50397184 | bytes 8520192 | tf_op jit(solution)/shard_map/nr,nmh->rmh/dot_general | solution.py:94
  231.9 13.4 %all_gather.13 = bf16[256,1024]{1,0:T(8,128)(2,1)S(1)} all-gather(bf16[256,256]{1,0:T(8,128)(2,1)S(1)} %bitcast.99), channel_id=1, replica_groups=mesh['paper'=64,'author'=4] {'author'}, dimensions={1}, use_global_device_ids=true | all-gather | bytes 655360 | tf_op jit(solution)/shard_map/all_gather | solution.py:138
  247.7 12.8 %all_gather.15 = bf16[256,1024]{1,0:T(8,128)(2,1)S(1)} all-gather(bf16[256,256]{1,0:T(8,128)(2,1)S(1)} %get-tuple-element.5), channel_id=1, replica_groups=mesh['paper'=64,'author'=4] {'author'}, dimensions={1}, use_global_device_ids=true | all-gather | bytes 655360 | tf_op jit(solution)/shard_map/all_gather | solution.py:152
  263.3 5.6 %fusion.11 = bf16[48,128,256]{1,2,0:T(8,128)(2,1)} fusion(f32[48]{0:T(128)S(1)} %copy-done.21, bf16[48,128,128]{2,1,0:T(8,128)(2,1)} %param.24, bf16[48,128,256]{2,1,0:T(8,128)(2,1)} %gather_fusion.3, pred[48]{0:T(512)(128)(4,1)S(1)} %copy-done.22), kind=kOutput, calls=%fused_computation.21 | convolution fusion | flops 407371776 | bytes 7864560 | tf_op jit(solution)/shard_map/pdg,pdw->pgw/dot_general | solution.py:163
  268.9 5.0 copy.72
  273.9 3.2 convert_bitcast_fusion.1
  277.1 4.4 copy.73
  281.5 10.6 %all-to-all-start.3 = ((bf16[64,1,128,256]{3,2,1,0:T(8,128)(2,1)}), bf16[64,1,128,256]{3,2,1,0:T(8,128)(2,1)}, u32[]{:S(2)}, u32[]{:S(2)}) async-start(bf16[64,1,128,256]{3,2,1,0:T(8,128)(2,1)} %copy.73), calls=%async_computation.3 | async-start | bytes 8388608 | tf_op jit(solution)/shard_map/all_to_all | solution.py:176
  295.6 4.3 fusion.23
  299.9 4.5 copy.77
  304.4 2.9 convert_bitcast_fusion
  307.4 4.4 copy.78
  311.8 76.6 %all-to-all-done.3 = bf16[64,1,128,256]{3,2,1,0:T(8,128)(2,1)} async-done(((bf16[64,1,128,256]{3,2,1,0:T(8,128)(2,1)}), bf16[64,1,128,256]{3,2,1,0:T(8,128)(2,1)}, u32[]{:S(2)}, u32[]{:S(2)}) %all-to-all-start.3) | async-done | bytes 4194336 | tf_op jit(solution)/shard_map/all_to_all | solution.py:176
  388.4 5.9 %all-to-all-start.4 = ((bf16[64,1,128,256]{3,2,1,0:T(8,128)(2,1)}), bf16[64,1,128,256]{3,2,1,0:T(8,128)(2,1)}, u32[]{:S(2)}, u32[]{:S(2)}) async-start(bf16[64,1,128,256]{3,2,1,0:T(8,128)(2,1)} %copy.78), calls=%async_computation.4 | async-start | bytes 8388608 | tf_op jit(solution)/shard_map/all_to_all | solution.py:205
  395.5 4.5 fusion.4
  401.1 89.4 %all-to-all-done.4 = bf16[64,1,128,256]{3,2,1,0:T(8,128)(2,1)} async-done(((bf16[64,1,128,256]{3,2,1,0:T(8,128)(2,1)}), bf16[64,1,128,256]{3,2,1,0:T(8,128)(2,1)}, u32[]{:S(2)}, u32[]{:S(2)}) %all-to-all-start.4) | async-done | bytes 4194336 | tf_op jit(solution)/shard_map/all_to_all | solution.py:205
  490.5 4.5 fusion.30
  (102 shorter events, 35.2 us)
Async XLA Ops:
  7.2 238.4 %copy-start = (bf16[1024,1024]{1,0:T(8,128)(2,1)S(1)}, bf16[1024,1024]{1,0:T(8,128)(2,1)}, u32[]{:S(2)}) copy-start(bf16[1024,1024]{1,0:T(8,128)(2,1)} %param.30) | copy-start | bytes 6291460
  7.2 25.9 %copy-start.1 = (bf16[256,256]{1,0:T(8,128)(2,1)S(1)}, bf16[256,256]{1,0:T(8,128)(2,1)}, u32[]{:S(2)}) copy-start(bf16[256,256]{1,0:T(8,128)(2,1)} %param.18) | copy-start | bytes 393220
  7.2 204.8 %all-gather.2.cloned.1.call-start = ((), (), s32[]{:S(2)}) async-start(), calls=%async_computation.5 | async-start | bytes 8519680 | tf_op jit(solution)/shard_map/all_gather | solution.py:85
  9.5 0.7 copy-start.10
  40.5 5.9 %copy-start.2 = (bf16[256,256]{1,0:T(8,128)(2,1)S(1)}, bf16[256,256]{1,0:T(8,128)(2,1)}, u32[]{:S(2)}) copy-start(bf16[256,256]{1,0:T(8,128)(2,1)} %param.17) | copy-start | bytes 393220
  40.5 8.1 %copy-start.15 = (s32[48,1]{0,1:T(1,128)S(1)}, s32[48,1]{0,1:T(1,128)}, u32[]{:S(2)}) copy-start(s32[48,1]{0,1:T(1,128)} %param.19) | copy-start | bytes 580
  40.5 8.3 %copy-start.16 = (s32[48]{0:T(128)S(1)}, s32[48]{0:T(128)}, u32[]{:S(2)}) copy-start(s32[48]{0:T(128)} %param.20) | copy-start | bytes 580
  40.5 8.9 %copy-start.19 = (s32[48]{0:T(128)S(1)}, s32[48]{0:T(128)}, u32[]{:S(2)}) copy-start(s32[48]{0:T(128)} %param.21) | copy-start | bytes 580
  40.5 9.5 %copy-start.17 = (s32[32]{0:T(128)S(1)}, s32[32]{0:T(128)}, u32[]{:S(2)}) copy-start(s32[32]{0:T(128)} %param.28) | copy-start | bytes 388
  40.5 10.1 %copy-start.14 = (s32[32,1]{0,1:T(1,128)S(1)}, s32[32,1]{0,1:T(1,128)}, u32[]{:S(2)}) copy-start(s32[32,1]{0,1:T(1,128)} %param.25) | copy-start | bytes 388
  40.5 122.1 %all-to-all-start.1 = ((bf16[64,1,128,256]{3,2,1,0:T(8,128)(2,1)}), bf16[64,1,128,256]{3,2,1,0:T(8,128)(2,1)}, u32[]{:S(2)}, u32[]{:S(2)}) async-start(bf16[64,1,128,256]{3,2,1,0:T(8,128)(2,1)} %bitcast_select_fusion), calls=%async_computation.1 | async-start | bytes 8388608 | tf_op jit(solution)/shard_map/all_to_all | solution.py:111
  46.3 9.0 %copy-start.18 = (s32[48]{0:T(128)S(1)}, s32[48]{0:T(128)}, u32[]{:S(2)}) copy-start(s32[48]{0:T(128)} %param.22) | copy-start | bytes 580
  46.3 9.0 %collective-permute-start = (bf16[256,256]{1,0:T(8,128)(2,1)S(1)}, bf16[256,256]{1,0:T(8,128)(2,1)S(1)}, u32[]{:S(2)}, u32[]{:S(2)}) collective-permute-start(bf16[256,256]{1,0:T(8,128)(2,1)S(1)} %copy-done.2), channel_id=1, source_target_pairs={{0,1},{1,2},{2,3},{3,0},{4,5},{5,6},{6,7},{7,4},{8,9},{9,10},{10,1... | collective-permute-start | bytes 393224 | tf_op jit(solution)/shard_map/ppermute | solution.py:132
  48.8 13.6 %copy-start.6 = (s32[48]{0:T(128)}, s32[48]{0:T(128)S(1)}, u32[]{:S(2)}) copy-start(s32[48]{0:T(128)S(1)} %fusion.81) | copy-start | bytes 580
  55.3 7.0 %copy-start.20 = (f32[48]{0:T(128)}, f32[48]{0:T(128)S(1)}, u32[]{:S(2)}) copy-start(f32[48]{0:T(128)S(1)} %compare_select_fusion.8) | copy-start | bytes 580
  55.4 5.1 %collective-permute-start.1 = (bf16[256,256]{1,0:T(8,128)(2,1)S(1)}, bf16[256,256]{1,0:T(8,128)(2,1)S(1)}, u32[]{:S(2)}, u32[]{:S(2)}) collective-permute-start(bf16[256,256]{1,0:T(8,128)(2,1)S(1)} %collective-permute-done), channel_id=1, source_target_pairs={{0,1},{1,2},{2,3},{3,0},{4,5},{5,6},{6,7},{7,4},{8,9},{9,10},{10,1... | collective-permute-start | bytes 393224 | tf_op jit(solution)/shard_map/ppermute | solution.py:132
  60.4 5.1 %collective-permute-start.2 = (bf16[256,256]{1,0:T(8,128)(2,1)S(1)}, bf16[256,256]{1,0:T(8,128)(2,1)}, u32[]{:S(2)}, u32[]{:S(2)}) collective-permute-start(bf16[256,256]{1,0:T(8,128)(2,1)S(1)} %collective-permute-done.1), channel_id=1, source_target_pairs={{0,1},{1,2},{2,3},{3,0},{4,5},{5,6},{6,7},{7,4},{8,9},{9,10},{10,1... | collective-permute-start | bytes 393224 | tf_op jit(solution)/shard_map/ppermute | solution.py:132
  63.2 119.8 %copy-start.3 = (bf16[32,128,128]{2,1,0:T(8,128)(2,1)S(1)}, bf16[32,128,128]{2,1,0:T(8,128)(2,1)}, u32[]{:S(2)}) copy-start(bf16[32,128,128]{2,1,0:T(8,128)(2,1)} %param.29) | copy-start | bytes 3145732
  162.6 118.9 %all-to-all-start.2 = ((s32[64,1,1]{2,1,0:T(1,128)}), s32[64,1,1]{2,1,0:T(1,128)S(1)}, u32[]{:S(2)}, u32[]{:S(2)}) async-start(s32[64,1,1]{2,1,0:T(1,128)} %copy.70), calls=%async_computation.2 | async-start | bytes 65536 | tf_op jit(solution)/shard_map/all_to_all | solution.py:70
  187.4 5.5 %copy-start.9 = (s32[32]{0:T(128)S(1)}, s32[32]{0:T(128)}, u32[]{:S(2)}) copy-start(s32[32]{0:T(128)} %param.26) | copy-start | bytes 388
  187.4 5.5 %copy-start.12 = (f32[32]{0:T(128)S(1)}, f32[32]{0:T(128)}, u32[]{:S(2)}) copy-start(f32[32]{0:T(128)} %convert_divide_fusion) | copy-start | bytes 388
  212.0 6.2 %copy-start.13 = (pred[64]{0:T(512)(128)(4,1)S(1)}, pred[64]{0:T(512)(128)(4,1)}, u32[]{:S(2)}) copy-start(pred[64]{0:T(512)(128)(4,1)} %compare_and_fusion.3) | copy-start | bytes 196
  218.1 5.1 %copy-start.8 = (f32[64,2,1]{0,1,2:T(2,128)S(1)}, f32[64,2,1]{0,1,2:T(2,128)}, u32[]{:S(2)}) copy-start(f32[64,2,1]{0,1,2:T(2,128)} %convolution_bitcast_fusion.1) | copy-start | bytes 1540
  223.2 22.0 %copy-start.4 = (bf16[1024,1024]{1,0:T(8,128)(2,1)S(1)}, bf16[1024,1024]{1,0:T(8,128)(2,1)}, u32[]{:S(2)}) copy-start(bf16[1024,1024]{1,0:T(8,128)(2,1)} %param.31) | copy-start | bytes 6291460
  223.2 22.3 %copy-start.5 = (bf16[256,256]{1,0:T(8,128)(2,1)S(1)}, bf16[256,256]{1,0:T(8,128)(2,1)}, u32[]{:S(2)}) copy-start(bf16[256,256]{1,0:T(8,128)(2,1)} %param.33) | copy-start | bytes 393220
  260.8 2.5 copy-start.21
  260.8 2.5 copy-start.22
  268.9 5.0 copy-start.7
  281.5 106.8 %all-to-all-start.3 = ((bf16[64,1,128,256]{3,2,1,0:T(8,128)(2,1)}), bf16[64,1,128,256]{3,2,1,0:T(8,128)(2,1)}, u32[]{:S(2)}, u32[]{:S(2)}) async-start(bf16[64,1,128,256]{3,2,1,0:T(8,128)(2,1)} %copy.73), calls=%async_computation.3 | async-start | bytes 8388608 | tf_op jit(solution)/shard_map/all_to_all | solution.py:176
  299.9 4.5 copy-start.11
  388.4 102.2 %all-to-all-start.4 = ((bf16[64,1,128,256]{3,2,1,0:T(8,128)(2,1)}), bf16[64,1,128,256]{3,2,1,0:T(8,128)(2,1)}, u32[]{:S(2)}, u32[]{:S(2)}) async-start(bf16[64,1,128,256]{3,2,1,0:T(8,128)(2,1)} %copy.78), calls=%async_computation.4 | async-start | bytes 8388608 | tf_op jit(solution)/shard_map/all_to_all | solution.py:205
Sparse Core Ops, SparseCore 0:
  10.8 133.2 all-gather.1
